TPU v7x, 32 devices: a whole 2x2x4 slice. The times are simulated.
32 devices in a mesh: freq: 8 (over y, x, core), src: 4 (over z).
Axes of the slice: x: 2, y: 2, z: 4, core: 2. Of those that a mesh axis runs over, the one named last changes fastest.
Arguments:
- focusing: bfloat16 [32, 1024, 2048], P('src', 'freq'), may hold values from -6 to 6
- direct: bfloat16 [32, 1024, 2048], P('src', 'freq'), may hold values from -6 to 6
- kernel: bfloat16 [2, 192, 2048, 1024], P(None, 'freq', 'src'), may hold values from -0.125 to 0.125
- onset_up: int32 [32, 2048], P('freq', 'src'), may hold values from 256 to 2048
- onset_back: int32 [32, 1024], P('src', 'freq'), may hold values from 256 to 2048
Outputs:
- upgoing: bfloat16 [32, 2048, 2048], P('freq', 'src')
- updated: bfloat16 [32, 1024, 2048], P('src', 'freq')
All inputs are finite; a program needn't handle non-finite values.
Results may differ from a plain program's by a relative error of at most 0.008.
Values may be sent and summed in bfloat16 or wider, within the bound.
A program may use at most 128 MiB of HBM per device.

v0:
```python
import math

import jax
import jax.numpy as jnp
from jax import lax
from jax.sharding import PartitionSpec as P

NT = 2048
NF = 192
BIN0 = 16


def frequency_band_tables():
    sample_index = jnp.arange(NT, dtype=jnp.int32)
    bin_index = BIN0 + jnp.arange(NF, dtype=jnp.int32)
    phase = sample_index[:, None] * bin_index[None, :] % NT
    angle = phase.astype(jnp.float32) * (2.0 * math.pi / NT)
    cosine = jnp.cos(angle)
    sine = jnp.sin(angle)
    forward_table = jnp.stack([cosine, -sine], axis=2).reshape(NT, 2 * NF).astype(jnp.bfloat16)
    inverse_table = (
        (2.0 / NT * jnp.stack([cosine.T, -sine.T], axis=1)).reshape(2 * NF, NT).astype(jnp.bfloat16)
    )
    return (forward_table, inverse_table)


def forward_waves(kernel_real_part, kernel_imaginary, spectrum):
    spectral_real = spectrum[:, 0]
    spectral_imaginary = spectrum[:, 1]
    wave_real = jnp.einsum(
        "izb,ijb->ijz", kernel_real_part, spectral_real, preferred_element_type=jnp.float32
    ) - jnp.einsum(
        "izb,ijb->ijz", kernel_imaginary, spectral_imaginary, preferred_element_type=jnp.float32
    )
    wave_imag = jnp.einsum(
        "izb,ijb->ijz", kernel_real_part, spectral_imaginary, preferred_element_type=jnp.float32
    ) + jnp.einsum(
        "izb,ijb->ijz", kernel_imaginary, spectral_real, preferred_element_type=jnp.float32
    )
    return jnp.stack([wave_real, wave_imag], axis=1).astype(jnp.bfloat16)


def adjoint_terms(kernel_real_part, kernel_imaginary, spectrum):
    backward_real = spectrum[:, 0]
    backward_imaginary = spectrum[:, 1]
    term_real = jnp.einsum(
        "doy,dvo->vdy", kernel_real_part, backward_real, preferred_element_type=jnp.float32
    ) + jnp.einsum(
        "doy,dvo->vdy", kernel_imaginary, backward_imaginary, preferred_element_type=jnp.float32
    )
    term_imag = jnp.einsum(
        "doy,dvo->vdy", kernel_real_part, backward_imaginary, preferred_element_type=jnp.float32
    ) - jnp.einsum(
        "doy,dvo->vdy", kernel_imaginary, backward_real, preferred_element_type=jnp.float32
    )
    return jnp.stack([term_real, term_imag], axis=2)


def local(focusing, direct, kernel, onset_up, onset_back):
    forward_table, inverse_table = frequency_band_tables()
    kernel_real_part = kernel[0]
    kernel_imaginary = kernel[1]
    sample_index = jnp.arange(NT, dtype=jnp.int32)
    point_count = focusing.shape[0]
    recv_count = focusing.shape[1]
    bins_local = jnp.einsum(
        "tk,prt->kpr", forward_table, focusing, preferred_element_type=jnp.float32
    )
    bins_local = bins_local.astype(jnp.bfloat16).reshape(NF, 2, point_count, recv_count)
    grouped = lax.all_to_all(bins_local, "freq", split_axis=0, concat_axis=3, tiled=True)
    waves = forward_waves(
        kernel_real_part, kernel_imaginary, lax.all_gather(grouped, "src", axis=2, tiled=True)
    )
    timed = lax.all_to_all(waves, "freq", split_axis=2, concat_axis=0, tiled=True)
    up_points = timed.shape[2]
    source_count = timed.shape[3]
    signal = jnp.einsum(
        "kps,kt->pst",
        timed.reshape(2 * NF, up_points, source_count),
        inverse_table,
        preferred_element_type=jnp.float32,
    )
    upgoing = jnp.where(sample_index[None, None, :] < onset_up[:, :, None], signal, 0.0).astype(
        jnp.bfloat16
    )
    back_local = jnp.einsum(
        "tk,pst->kps", forward_table, upgoing, preferred_element_type=jnp.float32
    )
    back_local = back_local.astype(jnp.bfloat16).reshape(NF, 2, up_points, source_count)
    banded = lax.all_to_all(back_local, "freq", split_axis=0, concat_axis=2, tiled=True)
    summed_band = lax.psum_scatter(
        adjoint_terms(kernel_real_part, kernel_imaginary, banded).astype(jnp.bfloat16),
        "src",
        scatter_dimension=0,
        tiled=True,
    )
    summed = lax.all_to_all(summed_band, "freq", split_axis=3, concat_axis=1, tiled=True)
    back_count = summed.shape[3]
    trace = jnp.einsum(
        "pkr,kt->prt",
        summed.reshape(point_count, 2 * NF, back_count),
        inverse_table,
        preferred_element_type=jnp.float32,
    )
    cut = jnp.where(sample_index[None, None, :] < onset_back[:, :, None], trace, 0.0)
    updated = (direct.astype(jnp.float32) - cut).astype(jnp.bfloat16)
    return (upgoing, updated)


def solution(mesh):
    placed = (
        P("src", "freq", None),
        P("src", "freq", None),
        P(None, "freq", "src", None),
        P("freq", "src"),
        P("src", "freq"),
    )
    return jax.shard_map(
        local,
        mesh=mesh,
        in_specs=placed,
        out_specs=(P("freq", "src", None), P("src", "freq", None)),
        check_vma=False,
    )
```

profile of v0, /device:TPU:0, one launch (start us, length us, event | category | flops | bytes accessed | tf_op | source)
XLA Modules:
  0.0 381.5 jit_solution(8613087912578638027)
XLA Ops:
  7.2 0.0 all-gather.2.cloned.1.call-start
  7.2 6.9 %cosine_convert_fusion = (bf16[2048,192,1]{0,1,2:T(8,128)(2,1)S(1)}, bf16[2048,192,1]{0,1,2:T(8,128)(2,1)S(1)}) fusion(s32[192]{0:T(256)S(1)} %iota_add_fusion), kind=kLoop, calls=%fused_computation.60 | loop fusion | flops 6684672 | bytes 1573632 | tf_op jit(solution)/shard_map/convert.10
  14.2 0.1 pad_maximum_fusion.1
  14.3 1.6 copy.59
  15.9 0.6 reshape.241
  16.6 4.7 %convolution_convert_fusion.1 = bf16[384,8,128]{2,0,1:T(8,128)(2,1)S(1)} fusion(bf16[2048,384,1]{0,1,2:T(8,128)(2,1)S(1)} %reshape.241, bf16[8,128,2048]{2,1,0:T(8,128)(2,1)} %param.5), kind=kOutput, calls=%fused_computation.65 | convolution fusion | flops 1611005952 | bytes 6553600 | tf_op jit(solution)/shard_map/tk,prt->kpr/dot_general | solution.py:66
  21.3 0.5 copy.60
  21.9 17.7 %all_to_all.66 = bf16[192,2,8,128]{3,1,2,0:T(2,128)(2,1)S(1)} all-to-all(bf16[192,2,8,128]{3,1,2,0:T(2,128)(2,1)S(1)} %copy.60), channel_id=1, replica_groups=mesh['freq'=8,'src'=4] {'freq'}, dimensions={0} | all-to-all | bytes 1572864 | tf_op jit(solution)/shard_map/all_to_all | solution.py:70
  39.6 1.1 copy.88
  40.7 0.0 all-gather.2.cloned.1.call-update
  40.7 63.0 %all-gather.2.cloned.1.call-done = bf16[24,2,32,1024]{3,2,0,1:T(8,128)(2,1)} async-done(((bf16[24,2,8,1024]{3,2,0,1:T(8,128)(2,1)}), bf16[24,2,32,1024]{3,2,0,1:T(8,128)(2,1)}) %all-gather.2.cloned.1.call-update) | async-done | bytes 3145744 | tf_op jit(solution)/shard_map/all_gather | solution.py:72
  103.7 13.8 %fusion.4 = f32[24,32,512]{2,1,0:T(8,128)} fusion(bf16[2,24,512,1024]{3,2,1,0:T(8,128)(2,1)} %param.7, bf16[24,2,32,1024]{3,2,0,1:T(8,128)(2,1)} %all-gather.2.cloned.1.call-done), kind=kOutput, calls=%fused_computation.4 | convolution fusion | flops 805306368 | bytes 28311552 | tf_op jit(solution)/shard_map/izb,ijb->ijz/dot_general | solution.py:37
  117.5 13.2 %fusion.6 = f32[24,32,512]{2,1,0:T(8,128)} fusion(bf16[2,24,512,1024]{3,2,1,0:T(8,128)(2,1)} %param.7, bf16[24,2,32,1024]{3,2,0,1:T(8,128)(2,1)S(1)} %copy-done.4), kind=kOutput, calls=%fused_computation.6 | convolution fusion | flops 805306368 | bytes 28311552 | tf_op jit(solution)/shard_map/izb,ijb->ijz/dot_general | solution.py:32
  130.7 13.0 %fusion.51 = bf16[24,1,32,512]{3,2,0,1:T(8,128)(2,1)S(1)} fusion(f32[24,32,512]{2,1,0:T(8,128)} %fusion.4, bf16[2,24,512,1024]{3,2,1,0:T(8,128)(2,1)} %param.7, bf16[24,2,32,1024]{3,2,0,1:T(8,128)(2,1)} %all-gather.2.cloned.1.call-done), kind=kOutput, calls=%fused_computation.67 | convolution fusion | flops 806092800 | bytes 29097984 | tf_op jit(solution)/shard_map/izb,ijb->ijz/dot_general | solution.py:35
  143.8 12.8 %fusion.46 = bf16[24,1,32,512]{3,2,0,1:T(8,128)(2,1)S(1)} fusion(f32[24,32,512]{2,1,0:T(8,128)S(1)} %copy-done.8, bf16[2,24,512,1024]{3,2,1,0:T(8,128)(2,1)} %param.7, bf16[24,2,32,1024]{3,2,0,1:T(8,128)(2,1)} %all-gather.2.cloned.1.call-done), kind=kOutput, calls=%fused_computation.66 | convolution fusion | flops 806092800 | bytes 29097984 | tf_op jit(solution)/shard_map/izb,ijb->ijz/dot_general | solution.py:30
  156.6 0.1 pad_maximum_fusion.2
  156.8 2.0 copy.62
  158.8 3.9 %all-to-all-start.1 = ((bf16[24,2,32,512]{3,0,1,2:T(8,128)(2,1)}), bf16[24,2,32,512]{3,0,1,2:T(8,128)(2,1)S(1)}, u32[]{:S(2)}, u32[]{:S(2)}) async-start(bf16[24,2,32,512]{3,0,1,2:T(8,128)(2,1)} %copy.62), calls=%async_computation.1 | async-start | bytes 3145728 | tf_op jit(solution)/shard_map/all_to_all | solution.py:74
  162.7 0.0 reduce-scatter.4.cloned.1.call-start
  162.7 6.2 %fusion.55 = (f32[192,1,2048]{2,0,1:T(8,128)S(1)}, f32[192,1,2048]{2,0,1:T(8,128)S(1)}) fusion(s32[192]{0:T(256)S(1)} %iota_add_fusion), kind=kLoop, calls=%fused_computation.72 | loop fusion | flops 5898240 | bytes 3146496 | tf_op jit(solution)/shard_map/cos | solution.py:18
  169.0 0.2 fusion.24
  169.2 1.6 copy.64
  170.8 2.5 reshape.242
  173.3 10.4 %all-to-all-done.1 = bf16[24,2,32,512]{3,0,1,2:T(8,128)(2,1)S(1)} async-done(((bf16[24,2,32,512]{3,0,1,2:T(8,128)(2,1)}), bf16[24,2,32,512]{3,0,1,2:T(8,128)(2,1)S(1)}, u32[]{:S(2)}, u32[]{:S(2)}) %all-to-all-start.1) | async-done | bytes 1572896 | tf_op jit(solution)/shard_map/all_to_all | solution.py:74
  183.7 1.2 copy.63
  184.9 0.2 copy-done.2
  185.1 5.0 %select_convert_fusion = bf16[4,512,2048]{2,1,0:T(8,128)(2,1)S(1)} fusion(s32[4,512]{1,0:T(4,128)S(1)} %copy-done.5, bf16[384,2048,1]{1,0,2:T(8,128)(2,1)S(1)} %copy-done.2, bf16[384,4,512]{2,1,0:T(4,128)(2,1)S(1)} %bitcast.122), kind=kOutput, calls=%fused_computation.16 | convolution fusion | flops 3233808384 | bytes 11542528 | tf_op jit(solution)/shard_map/kps,kt->pst/dot_general | solution.py:77
  190.1 3.4 copy-done.7
  193.5 3.5 convolution_convert_fusion
  197.0 0.6 reshape.239
  197.7 1.1 copy.66
  198.7 23.6 %all_to_all.67 = bf16[192,2,4,512]{3,1,2,0:T(2,128)(2,1)S(1)} all-to-all(bf16[192,2,4,512]{3,1,2,0:T(2,128)(2,1)S(1)} %copy.66), channel_id=1, replica_groups=mesh['freq'=8,'src'=4] {'freq'}, dimensions={0} | all-to-all | bytes 3145728 | tf_op jit(solution)/shard_map/all_to_all | solution.py:90
  222.3 0.9 copy.87
  223.2 0.4 all_to_all.58
  223.6 10.4 %fusion = f32[24,32,1024]{2,1,0:T(8,128)S(1)} fusion(bf16[2,24,512,1024]{3,2,1,0:T(8,128)(2,1)} %param.7, bf16[24,2,32,512]{3,2,0,1:T(8,128)(2,1)S(1)} %all_to_all.58), kind=kOutput, calls=%fused_computation | convolution fusion | flops 805306368 | bytes 29097984 | tf_op jit(solution)/shard_map/doy,dvo->vdy/dot_general | solution.py:53
  234.1 10.4 %fusion.2 = f32[24,32,1024]{2,1,0:T(8,128)S(1)} fusion(bf16[2,24,512,1024]{3,2,1,0:T(8,128)(2,1)} %param.7, bf16[24,2,32,512]{3,2,0,1:T(8,128)(2,1)S(1)} %all_to_all.58), kind=kOutput, calls=%fused_computation.2 | convolution fusion | flops 805306368 | bytes 29097984 | tf_op jit(solution)/shard_map/doy,dvo->vdy/dot_general | solution.py:48
  244.5 10.9 %fusion.32 = bf16[32,24,1,1024]{3,0,1,2:T(8,128)(2,1)S(1)} fusion(f32[24,32,1024]{2,1,0:T(8,128)S(1)} %fusion, bf16[2,24,512,1024]{3,2,1,0:T(8,128)(2,1)} %param.7, bf16[24,2,32,512]{3,2,0,1:T(8,128)(2,1)S(1)} %all_to_all.58), kind=kOutput, calls=%fused_computation.47 | convolution fusion | flops 806879232 | bytes 30670848 | tf_op jit(solution)/shard_map/doy,dvo->vdy/dot_general | solution.py:51
  255.4 10.9 %fusion.31 = bf16[32,24,1,1024]{3,0,1,2:T(8,128)(2,1)S(1)} fusion(f32[24,32,1024]{2,1,0:T(8,128)S(1)} %fusion.2, bf16[2,24,512,1024]{3,2,1,0:T(8,128)(2,1)} %param.7, bf16[24,2,32,512]{3,2,0,1:T(8,128)(2,1)S(1)} %all_to_all.58), kind=kOutput, calls=%fused_computation.46 | convolution fusion | flops 806879232 | bytes 30670848 | tf_op jit(solution)/shard_map/doy,dvo->vdy/dot_general | solution.py:46
  266.3 0.3 pad_maximum_fusion
  266.6 2.1 copy.77
  268.7 0.0 reduce-scatter.4.cloned.1.call-update
  268.7 57.3 %reduce-scatter.4.cloned.1.call-done = bf16[8,49152]{1,0:T(8,128)(2,1)} async-done(((bf16[32,49152]{1,0:T(8,128)(2,1)}), bf16[8,49152]{1,0:T(8,128)(2,1)}) %reduce-scatter.4.cloned.1.call-update) | async-done | bytes 786448
  326.0 7.1 %copy.68 = bf16[8,24,2,1024]{1,0,2,3:T(8,128)(2,1)} copy(bf16[8,24,2,1024]{3,0,1,2:T(8,128)(2,1)} %bitcast.123) | data formatting | bytes 1572864 | tf_op jit(solution)/shard_map/reduce_scatter | solution.py:91
  333.1 6.6 %reshape.247 = bf16[8,2,24576]{2,1,0:T(2,128)(2,1)S(1)} reshape(bf16[1024,2,8,24]{3,2,1,0:T(8,128)(2,1)} %bitcast.113) | data formatting | bytes 1572864
  339.7 16.2 %all_to_all.68 = bf16[8,2,24576]{2,1,0:T(2,128)(2,1)S(1)} all-to-all(bf16[8,2,24576]{2,1,0:T(2,128)(2,1)S(1)} %reshape.247), channel_id=1, replica_groups=mesh['freq'=8,'src'=4] {'freq'}, dimensions={0} | all-to-all | bytes 1572864 | tf_op jit(solution)/shard_map/all_to_all | solution.py:97
  355.9 6.9 %reshape.248 = bf16[1024,2,8,24]{3,2,1,0:T(8,128)(2,1)} reshape(bf16[8,2,24576]{2,1,0:T(2,128)(2,1)S(1)} %all_to_all.68) | data formatting | bytes 1572864
  362.8 5.4 %copy.70 = bf16[8,8,24,2,128]{4,0,3,2,1:T(8,128)(2,1)S(1)} copy(bf16[8,8,24,2,128]{2,0,3,4,1:T(8,128)(2,1)} %bitcast.114) | data formatting | bytes 1572864 | tf_op jit(solution)/shard_map/all_to_all | solution.py:97
  368.2 6.3 %subtract_convert_fusion = bf16[8,128,2048]{2,1,0:T(8,128)(2,1)} fusion(bf16[8,128,2048]{2,1,0:T(8,128)(2,1)} %param.6, bf16[384,2048,1]{1,0,2:T(8,128)(2,1)S(1)} %copy-done.3, s32[8,128]{1,0:T(8,128)S(1)} %copy-done.6, bf16[8,384,128]{2,0,1:T(8,128)(2,1)S(1)} %bitcast.124), kind=kOutput, calls=%fused_computation.26 | convolution fusion | flops 1621098496 | bytes 10752000 | tf_op jit(solution)/shard_map/pkr,kt->prt/dot_general | solution.py:99
  (17 shorter events, 0.0 us)
Async XLA Ops:
  7.2 96.5 %all-gather.2.cloned.1.call-start = ((), (), s32[]{:S(2)}) async-start(), calls=%async_computation.5 | async-start | bytes 3932160 | tf_op jit(solution)/shard_map/all_gather | solution.py:72
  16.6 4.7 %copy-start = (bf16[2048,384,1]{0,1,2:T(8,128)(2,1)}, bf16[2048,384,1]{0,1,2:T(8,128)(2,1)S(1)}, u32[]{:S(2)}) copy-start(bf16[2048,384,1]{0,1,2:T(8,128)(2,1)S(1)} %reshape.241) | copy-start | bytes 4718596
  103.7 13.8 %copy-start.4 = (bf16[24,2,32,1024]{3,2,0,1:T(8,128)(2,1)S(1)}, bf16[24,2,32,1024]{3,2,0,1:T(8,128)(2,1)}, u32[]{:S(2)}) copy-start(bf16[24,2,32,1024]{3,2,0,1:T(8,128)(2,1)} %all-gather.2.cloned.1.call-done) | copy-start | bytes 9437188
  130.7 13.0 %copy-start.8 = (f32[24,32,512]{2,1,0:T(8,128)S(1)}, f32[24,32,512]{2,1,0:T(8,128)}, u32[]{:S(2)}) copy-start(f32[24,32,512]{2,1,0:T(8,128)} %fusion.6) | copy-start | bytes 4718596
  158.8 24.9 %all-to-all-start.1 = ((bf16[24,2,32,512]{3,0,1,2:T(8,128)(2,1)}), bf16[24,2,32,512]{3,0,1,2:T(8,128)(2,1)S(1)}, u32[]{:S(2)}, u32[]{:S(2)}) async-start(bf16[24,2,32,512]{3,0,1,2:T(8,128)(2,1)} %copy.62), calls=%async_computation.1 | async-start | bytes 3145728 | tf_op jit(solution)/shard_map/all_to_all | solution.py:74
  162.7 163.3 %reduce-scatter.4.cloned.1.call-start = ((), (), s32[]{:S(2)}) async-start(), calls=%async_computation.6 | async-start | bytes 3932160
  183.7 1.4 copy-start.2
  183.7 1.4 copy-start.5
  185.1 8.4 %copy-start.1 = (bf16[2048,384,1]{0,1,2:T(8,128)(2,1)S(1)}, bf16[2048,384,1]{0,1,2:T(8,128)(2,1)}, u32[]{:S(2)}) copy-start(bf16[2048,384,1]{0,1,2:T(8,128)(2,1)} %copy-done) | copy-start | bytes 4718596
  190.1 3.4 copy-start.7
  362.8 5.4 %copy-start.3 = (bf16[384,2048,1]{1,0,2:T(8,128)(2,1)S(1)}, bf16[384,2048,1]{1,0,2:T(8,128)(2,1)}, u32[]{:S(2)}) copy-start(bf16[384,2048,1]{1,0,2:T(8,128)(2,1)} %reshape.242) | copy-start | bytes 4718596
  362.8 5.4 %copy-start.6 = (s32[8,128]{1,0:T(8,128)S(1)}, s32[8,128]{1,0:T(8,128)}, u32[]{:S(2)}) copy-start(s32[8,128]{1,0:T(8,128)} %param.9) | copy-start | bytes 12292
Sparse Core Ops, SparseCore 0:
  40.8 62.8 all-gather.1
  268.8 57.1 reduce-scatter.3
where the time goes:
time: 387 us; the launch traced here: 382 us
  waiting for transfers between devices  131 us (34%)
  matrix products  115 us (30%)
  blocking collectives  57.6 us (15%)
  local copies, waits for them, and re-layouts  45.9 us (12%)
  between operations  14.5 us (4%)
  other arithmetic  14 us (4%)
  starting transfers between devices  3.98 us (1%)
    all_gather x1, waiting for transfers between devices, local(): lax.all_gather(grouped, 'src', axis=2, tiled=True)  63 us
    unnamed x3, waiting for transfers between devices  57.3 us
    all_to_all x1, blocking collectives, local(): lax.all_to_all(back_local, 'freq', split_axis=0, concat_axis=2, tiled=True)  23.6 us
    unnamed x21, local copies, waits for them, and re-layouts  19.2 us
    all_to_all x1, blocking collectives, local(): lax.all_to_all(bins_local, 'freq', split_axis=0, concat_axis=3, tiled=True)  17.7 us
    all_to_all x1, blocking collectives, local(): lax.all_to_all(summed_band, 'freq', split_axis=3, concat_axis=1, tiled=True)  16.2 us
    dot_general x1, matrix products, forward_waves(): jnp.einsum('izb,ijb->ijz', kernel_imaginary, spectral_real, preferred_ele...  13.8 us
    dot_general x1, matrix products, forward_waves(): jnp.einsum('izb,ijb->ijz', kernel_imaginary, spectral_imaginary, preferre...  13.2 us
  transfers between devices with their start and end apart: 3, of which 3 were waited for; matrix products, arithmetic and copies ran while one was open for 3% of the time, Pallas kernels for 0%

commit v1 on v0

v1 whole, which is shorter than its diff:
```python
import math

import jax
import jax.numpy as jnp
import ml_dtypes
import numpy as np
from jax import lax
from jax.experimental import pallas as pl
from jax.experimental.pallas import tpu as pltpu
from jax.sharding import PartitionSpec as P

BIN0 = 16


def band_tables(nt, nf):
    phase = np.arange(nt)[:, None] * (BIN0 + np.arange(nf))[None, :] % nt
    angle = phase.astype(np.float32) * np.float32(2.0 * math.pi / nt)
    both = np.stack([np.cos(angle), -np.sin(angle)], axis=2).reshape(nt, 2 * nf)
    both = both.astype(np.float32).T
    forward = both.astype(ml_dtypes.bfloat16)
    inverse = (np.float32(2.0 / nt) * both).astype(ml_dtypes.bfloat16)
    return np.ascontiguousarray(forward), np.ascontiguousarray(inverse)


NN = (((1,), (0,)), ((), ()))
NT_ = (((1,), (1,)), ((), ()))


def waves_kernel(pz, pf, spec_ref, kernel_ref, out_ref):
    nz, nf = spec_ref.shape[0], spec_ref.shape[1]
    x = jnp.concatenate(
        [
            jnp.concatenate([spec_ref[z, f, 0] for f in range(nf)], axis=1)
            for z in range(nz)
        ],
        axis=0,
    )
    a = lax.dot_general(x, kernel_ref[0, 0], NT_, preferred_element_type=jnp.float32)
    b = lax.dot_general(x, kernel_ref[1, 0], NT_, preferred_element_type=jnp.float32)
    for z in range(nz):
        r0, r1, r2 = 2 * z * pz, 2 * z * pz + pz, 2 * z * pz + 2 * pz
        real = a[r0:r1] - b[r1:r2]
        imag = a[r1:r2] + b[r0:r1]
        for h in range(pz // pf):
            rows = jnp.concatenate([real[h * pf : (h + 1) * pf], imag[h * pf : (h + 1) * pf]], axis=0)
            out_ref[z * (pz // pf) + h, 0] = rows.astype(jnp.bfloat16)


def terms_kernel(pz, pf, back_ref, kernel_ref, out_ref):
    nf = back_ref.shape[0]
    nz, rl = out_ref.shape[0], out_ref.shape[4]
    each = [back_ref[f, 0].astype(jnp.float32) for f in range(nf)]
    x = jnp.concatenate(
        [e[:pf] for e in each] + [e[pf:] for e in each], axis=0
    ).astype(jnp.bfloat16)
    half = nf * pf
    a = lax.dot_general(x, kernel_ref[0, 0], NN, preferred_element_type=jnp.float32)
    b = lax.dot_general(x, kernel_ref[1, 0], NN, preferred_element_type=jnp.float32)
    real = a[:half] + b[half:]
    imag = a[half:] - b[:half]
    for z in range(nz):
        rows = jnp.concatenate([real[z * pz : (z + 1) * pz], imag[z * pz : (z + 1) * pz]], axis=0)
        rows = rows.astype(jnp.bfloat16)
        for f in range(nf):
            out_ref[z, f, 0] = rows[:, f * rl : (f + 1) * rl]


def local(nf, nz, focusing, direct, kernel, onset_up, onset_back):
    pz, rl, nt = focusing.shape
    _, bins, sl, receivers = kernel.shape
    pf = onset_up.shape[0]
    forward, inverse = band_tables(nt, nf * bins)
    forward, inverse = jnp.asarray(forward), jnp.asarray(inverse)
    sample_index = jnp.arange(nt, dtype=jnp.int32)
    k_spec = pl.BlockSpec((2, 1, sl, receivers), lambda j: (0, j, 0, 0))
    params = pltpu.CompilerParams(vmem_limit_bytes=32 << 20)
    cost = pl.CostEstimate(
        flops=8 * bins * sl * receivers * nf * pf,
        bytes_accessed=4 * bins * sl * receivers,
        transcendentals=0,
    )

    spectrum = jnp.einsum("kt,prt->kpr", forward, focusing, preferred_element_type=jnp.float32)
    spectrum = spectrum.astype(jnp.bfloat16).reshape(nf, bins, 2 * pz, rl)
    grouped = lax.all_to_all(spectrum, "freq", split_axis=0, concat_axis=0, tiled=True)
    gathered = lax.all_gather(grouped, "src", axis=0, tiled=False)
    waves = pl.pallas_call(
        lambda *refs: waves_kernel(pz, pf, *refs),
        out_shape=jax.ShapeDtypeStruct((nf, bins, 2 * pf, sl), jnp.bfloat16),
        grid=(bins,),
        in_specs=[pl.BlockSpec((nz, nf, 1, 2 * pz, rl), lambda j: (0, 0, j, 0, 0)), k_spec],
        out_specs=pl.BlockSpec((nf, 1, 2 * pf, sl), lambda j: (0, j, 0, 0)),
        compiler_params=params,
        cost_estimate=cost,
        name="waves",
    )(gathered, kernel)
    timed = lax.all_to_all(waves, "freq", split_axis=0, concat_axis=0, tiled=True)
    signal = jnp.einsum(
        "kps,kt->pst",
        timed.reshape(2 * nf * bins, pf, sl),
        inverse,
        preferred_element_type=jnp.float32,
    )
    upgoing = jnp.where(sample_index[None, None, :] < onset_up[:, :, None], signal, 0.0).astype(
        jnp.bfloat16
    )
    back = jnp.einsum("kt,pst->kps", forward, upgoing, preferred_element_type=jnp.float32)
    back = back.astype(jnp.bfloat16).reshape(nf, bins, 2 * pf, sl)
    banded = lax.all_to_all(back, "freq", split_axis=0, concat_axis=0, tiled=True)
    terms = pl.pallas_call(
        lambda *refs: terms_kernel(pz, pf, *refs),
        out_shape=jax.ShapeDtypeStruct((nz, nf, bins, 2 * pz, rl), jnp.bfloat16),
        grid=(bins,),
        in_specs=[pl.BlockSpec((nf, 1, 2 * pf, sl), lambda j: (0, j, 0, 0)), k_spec],
        out_specs=pl.BlockSpec((nz, nf, 1, 2 * pz, rl), lambda j: (0, 0, j, 0, 0)),
        compiler_params=params,
        cost_estimate=cost,
        name="terms",
    )(banded, kernel)
    summed = lax.psum_scatter(terms, "src", scatter_dimension=0, tiled=False)
    spread = lax.all_to_all(summed, "freq", split_axis=0, concat_axis=0, tiled=True)
    trace = jnp.einsum(
        "kpr,kt->prt",
        spread.reshape(2 * nf * bins, pz, rl),
        inverse,
        preferred_element_type=jnp.float32,
    )
    cut = jnp.where(sample_index[None, None, :] < onset_back[:, :, None], trace, 0.0)
    updated = (direct.astype(jnp.float32) - cut).astype(jnp.bfloat16)
    return (upgoing, updated)


def solution(mesh):
    placed = (
        P("src", "freq", None),
        P("src", "freq", None),
        P(None, "freq", "src", None),
        P("freq", "src"),
        P("src", "freq"),
    )
    nf, nz = mesh.shape["freq"], mesh.shape["src"]
    return jax.shard_map(
        lambda *args: local(nf, nz, *args),
        mesh=mesh,
        in_specs=placed,
        out_specs=(P("freq", "src", None), P("src", "freq", None)),
        check_vma=False,
    )
```

time: 387 us -> 302 us (0.78); the launches traced: 382 us -> 301 us
  matrix products: 115 us -> 20.7 us
  Pallas kernels: 0 us -> 59.4 us
  local copies, waits for them, and re-layouts: 45.9 us -> 4.47 us
  blocking collectives: 57.6 us -> 81.7 us
  other arithmetic: 14 us -> 0 us
  waiting for transfers between devices: 131 us -> 120 us
  starting transfers between devices: 3.98 us -> 0.08 us
    dot_general x12 -> x4, matrix products: 115 us -> 20.7 us  [the longest x1 6.56 us: local(): jnp.einsum('kps,kt->pst', timed.reshape(2 * nf * bins, pf, sl), inverse,...]
    pallas_call x0 -> x2, Pallas kernels: none -> 59.4 us  [the longest x1 30.8 us: local(): pl.pallas_call(lambda *refs: waves_kernel(pz, pf, *refs), out_shape=jax.S...]
    unnamed x3 -> x2, waiting for transfers between devices: 57.3 us -> 0.03 us
    reduce_scatter x0 -> x1, waiting for transfers between devices: none -> 57.2 us  [local(): summed = lax.psum_scatter(terms, 'src', scatter_dimension=0, tiled=False)]
    all_to_all x3 -> x4, blocking collectives: 57.6 us -> 81.7 us  [the longest x1 24.4 us: local(): lax.all_to_all(waves, 'freq', split_axis=0, concat_axis=0, tiled=True)]
    unnamed x21 -> x12, local copies, waits for them, and re-layouts: 19.2 us -> 1.92 us
    all_to_all x1 -> x0, waiting for transfers between devices: 10.4 us -> none  [local(): lax.all_to_all(waves, 'freq', split_axis=2, concat_axis=0, tiled=True)]
    all_to_all x5 -> x0, local copies, waits for them, and re-layouts: 8.94 us -> none  [the longest x1 5.37 us: local(): lax.all_to_all(summed_band, 'freq', split_axis=3, concat_axis=1, tiled=True)]
  transfers between devices with their start and end apart: 3 -> 2, of which waited for: 3 -> 2; matrix products, arithmetic and copies ran while one was open for 3% -> 0% of each run, Pallas kernels for 0% -> 0%
where the time goes in v1:
time: 302 us; the launch traced here: 301 us
  waiting for transfers between devices  120 us (40%)
  blocking collectives  81.7 us (27%)
  Pallas kernels  59.4 us (20%)
  matrix products  20.7 us (7%)
  between operations  14.1 us (5%)
  local copies, waits for them, and re-layouts  4.47 us (1%)
    all_gather x1, waiting for transfers between devices, local(): gathered = lax.all_gather(grouped, 'src', axis=0, tiled=False)  63 us
    reduce_scatter x1, waiting for transfers between devices, local(): summed = lax.psum_scatter(terms, 'src', scatter_dimension=0, tiled=False)  57.2 us
    pallas_call x1, Pallas kernels, local(): pl.pallas_call(lambda *refs: waves_kernel(pz, pf, *refs), out_shape=jax.S...  30.8 us
    pallas_call x1, Pallas kernels, local(): pl.pallas_call(lambda *refs: terms_kernel(pz, pf, *refs), out_shape=jax.S...  28.6 us
    all_to_all x1, blocking collectives, local(): lax.all_to_all(waves, 'freq', split_axis=0, concat_axis=0, tiled=True)  24.4 us
    all_to_all x1, blocking collectives, local(): lax.all_to_all(back, 'freq', split_axis=0, concat_axis=0, tiled=True)  23.4 us
    all_to_all x1, blocking collectives, local(): lax.all_to_all(spectrum, 'freq', split_axis=0, concat_axis=0, tiled=True)  17.6 us
    all_to_all x1, blocking collectives, local(): lax.all_to_all(summed, 'freq', split_axis=0, concat_axis=0, tiled=True)  16.2 us
  transfers between devices with their start and end apart: 2, of which 2 were waited for; matrix products, arithmetic and copies ran while one was open for 0% of the time, Pallas kernels for 0%

profile of v1, /device:TPU:0, one launch (start us, length us, event | category | flops | bytes accessed | tf_op | source)
XLA Modules:
  0.0 300.7 jit_solution(17656889944524463432)
XLA Ops:
  7.2 0.0 all-gather.3.cloned.1.call-start
  7.2 4.5 %convolution_convert_fusion.1 = bf16[384,8,128]{2,0,1:T(8,128)(2,1)S(1)} fusion(bf16[384,2048,1]{1,0,2:T(8,128)(2,1)} %constant.9, bf16[8,128,2048]{2,1,0:T(8,128)(2,1)} %param.7), kind=kOutput, calls=%fused_computation.7 | convolution fusion | flops 1611005952 | bytes 6553600 | tf_op jit(solution)/shard_map/kt,prt->kpr/dot_general | solution.py:83
  11.7 0.5 copy.16
  12.2 17.6 %all_to_all.20 = bf16[8,24,16,128]{3,2,1,0:T(8,128)(2,1)} all-to-all(bf16[8,24,16,128]{3,2,1,0:T(8,128)(2,1)S(1)} %bitcast.17), channel_id=1, replica_groups=mesh['freq'=8,'src'=4] {'freq'}, dimensions={0} | all-to-all | bytes 1572864 | tf_op jit(solution)/shard_map/all_to_all | solution.py:85
  29.9 0.0 all-gather.3.cloned.1.call-update
  29.9 0.0 reduce-scatter.2.cloned.1.call-start
  29.9 63.0 %all-gather.3.cloned.1.call-done = bf16[32,24,16,128]{3,2,1,0:T(8,128)(2,1)} async-done(((bf16[8,24,16,128]{3,2,1,0:T(8,128)(2,1)}), bf16[32,24,16,128]{3,2,1,0:T(8,128)(2,1)}) %all-gather.3.cloned.1.call-update) | async-done | bytes 3145744 | tf_op jit(solution)/shard_map/all_gather | solution.py:86
  92.9 0.0 copy-start
  92.9 1.9 copy-done
  94.8 30.8 %waves.1 = bf16[8,24,8,512]{3,2,1,0:T(8,128)(2,1)S(1)} custom-call(bf16[4,8,24,16,128]{4,3,2,1,0:T(8,128)(2,1)S(1)} %bitcast.16, bf16[2,24,512,1024]{3,2,1,0:T(8,128)(2,1)} %refs_1_.3), custom_call_target="tpu_custom_call" | custom-call | flops 3221225472 | bytes 50331648 | tf_op jit(solution)/shard_map/waves/pallas_call | solution.py:87
  125.6 0.0 copy-start.1
  125.6 24.4 %all_to_all.21 = bf16[8,24,8,512]{3,2,1,0:T(8,128)(2,1)S(1)} all-to-all(bf16[8,24,8,512]{3,2,1,0:T(8,128)(2,1)S(1)} %waves.1), channel_id=1, replica_groups=mesh['freq'=8,'src'=4] {'freq'}, dimensions={0} | all-to-all | bytes 3145728 | tf_op jit(solution)/shard_map/all_to_all | solution.py:97
  150.0 0.4 reshape.19
  150.5 0.0 copy-done.1
  150.5 0.0 copy-start.5
  150.5 6.6 %select_convert_fusion = bf16[4,512,2048]{2,1,0:T(8,128)(2,1)S(1)} fusion(s32[4,512]{1,0:T(4,128)S(1)} %copy-done.1, bf16[384,2048,1]{1,0,2:T(8,128)(2,1)} %constant.10, bf16[384,4,512]{2,1,0:T(4,128)(2,1)S(1)} %reshape.19), kind=kOutput, calls=%fused_computation | convolution fusion | flops 3233808384 | bytes 11542528 | tf_op jit(solution)/shard_map/kps,kt->pst/dot_general | solution.py:98
  157.0 0.0 copy-done.5
  157.1 0.0 copy-start.3
  157.1 3.4 %fusion.1 = bf16[384,4,512]{2,0,1:T(8,128)(2,1)S(1)} fusion(bf16[4,512,2048]{2,1,0:T(8,128)(2,1)S(1)} %select_convert_fusion, bf16[384,2048,1]{1,0,2:T(8,128)(2,1)S(1)} %copy-done.5), kind=kOutput, calls=%fused_computation.6 | convolution fusion | flops 3222011904 | bytes 11534336 | tf_op jit(solution)/shard_map/kt,pst->kps/dot_general | solution.py:107
  160.5 0.0 copy-done.3
  160.5 1.2 copy.18
  161.8 0.4 reshape.20
  162.2 23.4 %all_to_all.22.refs_0_ = bf16[8,24,8,512]{3,2,1,0:T(8,128)(2,1)S(1)} all-to-all(bf16[8,24,8,512]{3,2,1,0:T(8,128)(2,1)S(1)} %reshape.20), channel_id=1, replica_groups=mesh['freq'=8,'src'=4] {'freq'}, dimensions={0} | all-to-all | bytes 3145728 | tf_op jit(solution)/shard_map/all_to_all | solution.py:109
  185.6 28.6 %terms.1 = bf16[4,8,24,16,128]{4,3,2,1,0:T(8,128)(2,1)} custom-call(bf16[8,24,8,512]{3,2,1,0:T(8,128)(2,1)S(1)} %all_to_all.22.refs_0_, bf16[2,24,512,1024]{3,2,1,0:T(8,128)(2,1)} %refs_1_.3), custom_call_target="tpu_custom_call" | custom-call | flops 3221225472 | bytes 50331648 | tf_op jit(solution)/shard_map/terms/pallas_call | solution.py:110
  214.2 0.0 copy-start.2
  214.2 0.0 copy-start.4
  214.2 0.0 reduce-scatter.2.cloned.1.call-update
  214.2 57.2 %reduce-scatter.2.cloned.1.call-done = bf16[1,8,24,16,128]{4,3,2,1,0:T(8,128)(2,1)} async-done(((bf16[4,8,24,16,128]{4,3,2,1,0:T(8,128)(2,1)}), bf16[1,8,24,16,128]{4,3,2,1,0:T(8,128)(2,1)}) %reduce-scatter.2.cloned.1.call-update) | async-done | bytes 786448 | tf_op jit(solution)/shard_map/reduce_scatter | solution.py:120
  271.5 16.2 %all_to_all.23 = bf16[8,24,16,128]{3,2,1,0:T(8,128)(2,1)S(1)} all-to-all(bf16[8,24,16,128]{3,2,1,0:T(8,128)(2,1)} %bitcast.18), channel_id=1, replica_groups=mesh['freq'=8,'src'=4] {'freq'}, dimensions={0} | all-to-all | bytes 1572864 | tf_op jit(solution)/shard_map/all_to_all | solution.py:121
  287.7 0.0 copy-done.2
  287.7 0.0 copy-done.4
  287.7 6.2 %subtract_convert_fusion = bf16[8,128,2048]{2,1,0:T(8,128)(2,1)} fusion(bf16[8,128,2048]{2,1,0:T(8,128)(2,1)} %param.8, bf16[384,2048,1]{1,0,2:T(8,128)(2,1)S(1)} %copy-done.4, s32[8,128]{1,0:T(8,128)S(1)} %copy-done.2, bf16[384,8,128]{2,1,0:T(8,128)(2,1)S(1)} %bitcast.19), kind=kOutput, calls=%fused_computation.2 | convolution fusion | flops 1621098496 | bytes 10752000 | tf_op jit(solution)/shard_map/kpr,kt->prt/dot_general | solution.py:122
Async XLA Ops:
  7.2 85.7 %all-gather.3.cloned.1.call-start = ((), (), s32[]{:S(2)}) async-start(), calls=%async_computation.6 | async-start | bytes 3932160 | tf_op jit(solution)/shard_map/all_gather | solution.py:86
  29.9 241.6 %reduce-scatter.2.cloned.1.call-start = ((), (), s32[]{:S(2)}) async-start(), calls=%async_computation.5 | async-start | bytes 3932160 | tf_op jit(solution)/shard_map/reduce_scatter | solution.py:120
  92.9 1.9 copy-start
  125.6 24.8 %copy-start.1 = (s32[4,512]{1,0:T(4,128)S(1)}, s32[4,512]{1,0:T(4,128)}, u32[]{:S(2)}) copy-start(s32[4,512]{1,0:T(4,128)} %param.10) | copy-start | bytes 24580
  150.5 6.6 %copy-start.5 = (bf16[384,2048,1]{1,0,2:T(8,128)(2,1)S(1)}, bf16[384,2048,1]{1,0,2:T(8,128)(2,1)}, u32[]{:S(2)}) copy-start(bf16[384,2048,1]{1,0,2:T(8,128)(2,1)} %constant.9) | copy-start | bytes 4718596
  157.1 3.5 %copy-start.3 = (bf16[4,512,2048]{2,1,0:T(8,128)(2,1)}, bf16[4,512,2048]{2,1,0:T(8,128)(2,1)S(1)}, u32[]{:S(2)}) copy-start(bf16[4,512,2048]{2,1,0:T(8,128)(2,1)S(1)} %select_convert_fusion) | copy-start | bytes 25165828
  214.2 73.5 %copy-start.2 = (s32[8,128]{1,0:T(8,128)S(1)}, s32[8,128]{1,0:T(8,128)}, u32[]{:S(2)}) copy-start(s32[8,128]{1,0:T(8,128)} %param.11) | copy-start | bytes 12292
  214.2 73.5 %copy-start.4 = (bf16[384,2048,1]{1,0,2:T(8,128)(2,1)S(1)}, bf16[384,2048,1]{1,0,2:T(8,128)(2,1)}, u32[]{:S(2)}) copy-start(bf16[384,2048,1]{1,0,2:T(8,128)(2,1)} %constant.10) | copy-start | bytes 4718596
Sparse Core Ops, SparseCore 0:
  30.0 62.8 all-gather.2
  214.4 57.0 reduce-scatter.1

commit v2 on v1

v2 whole, which is shorter than its diff:
```python
import math

import jax
import jax.numpy as jnp
import ml_dtypes
import numpy as np
from jax import lax
from jax.experimental import pallas as pl
from jax.experimental.pallas import tpu as pltpu
from jax.sharding import PartitionSpec as P

BIN0 = 16


def band_tables(nt, nf):
    phase = np.arange(nt)[:, None] * (BIN0 + np.arange(nf))[None, :] % nt
    angle = phase.astype(np.float32) * np.float32(2.0 * math.pi / nt)
    both = np.stack([np.cos(angle), -np.sin(angle)], axis=2).reshape(nt, 2 * nf)
    both = both.astype(np.float32).T
    forward = both.astype(ml_dtypes.bfloat16)
    inverse = (np.float32(2.0 / nt) * both).astype(ml_dtypes.bfloat16)
    return np.ascontiguousarray(forward), np.ascontiguousarray(inverse)


NN = (((1,), (0,)), ((), ()))
NT_ = (((1,), (1,)), ((), ()))


MESH = pl.DeviceIdType.MESH
LAG = 2
SLOTS = 3


def chunk_bins(bins):
    return 2 if bins % 2 == 0 else 1


def enter(f, z, nf, nz):
    barrier = pltpu.get_barrier_semaphore()
    for step in range(1, nf):
        pl.semaphore_signal(barrier, inc=1, device_id={"freq": lax.rem(f + step, nf)}, device_id_type=MESH)

    @pl.when(z > 0)
    def _():
        pl.semaphore_signal(barrier, inc=1, device_id={"src": z - 1}, device_id_type=MESH)

    @pl.when(z < nz - 1)
    def _():
        pl.semaphore_signal(barrier, inc=1, device_id={"src": z + 1}, device_id_type=MESH)

    near = jnp.where(z > 0, 1, 0) + jnp.where(z < nz - 1, 1, 0)
    pl.semaphore_wait(barrier, nf - 1 + near)


def remote(src, dst, send, recv, axis, index):
    return pltpu.make_async_remote_copy(
        src_ref=src, dst_ref=dst, send_sem=send, recv_sem=recv, device_id={axis: index}, device_id_type=MESH
    )


def settle(ref, sem):
    pltpu.make_async_copy(ref, ref, sem).wait()


def fetch(kern, kbuf, ksem, j):
    slot = lax.rem(j, SLOTS)
    return pltpu.make_async_copy(kern.at[:, j], kbuf.at[slot], ksem.at[slot])


def waves_kernel(
    nf, nz, pz, pf, spec, kern, out, gat, own, kbuf, ksem, lsem, osem, a_send, a_recv, z_send, z_recv, w_send, w_recv
):
    f, z = lax.axis_index("freq"), lax.axis_index("src")
    bins = spec.shape[1]
    chunk = chunk_bins(bins)
    count = bins // chunk

    def part(c):
        return pl.ds(c * chunk, chunk)

    for j in range(SLOTS):
        fetch(kern, kbuf, ksem, j).start()
    mine = pltpu.make_async_copy(spec.at[f], gat.at[z, f], lsem)
    mine.start()
    enter(f, z, nf, nz)

    def scatter(c, carry):
        for step in range(1, nf):
            t = lax.rem(f + step, nf)
            remote(
                spec.at[t, part(c)], gat.at[z, f, part(c)], a_send.at[step], a_recv.at[c], "freq", t
            ).start()
        return carry

    lax.fori_loop(0, count, scatter, 0)
    mine.wait()

    def pass_on(s, c, right):
        to = z + 1 if right else z - 1
        fits = z < nz - 1 if right else z > 0

        @pl.when(fits)
        def _():
            block = gat.at[s, :, part(c)]
            remote(block, block, z_send.at[0 if right else 1, s], z_recv.at[s, c], "src", to).start()

    def multiply(j):
        fetch(kern, kbuf, ksem, j).wait()
        slot = lax.rem(j, SLOTS)
        x = jnp.concatenate(
            [jnp.concatenate([gat[s, r, j] for r in range(nf)], axis=1) for s in range(nz)], axis=0
        )
        a = lax.dot_general(x, kbuf[slot, 0], NT_, preferred_element_type=jnp.float32)
        b = lax.dot_general(x, kbuf[slot, 1], NT_, preferred_element_type=jnp.float32)
        for s in range(nz):
            r0, r1, r2 = 2 * s * pz, 2 * s * pz + pz, 2 * s * pz + 2 * pz
            real = a[r0:r1] - b[r1:r2]
            imag = a[r1:r2] + b[r0:r1]
            for h in range(pz // pf):
                rows = jnp.concatenate([real[h * pf : (h + 1) * pf], imag[h * pf : (h + 1) * pf]], axis=0)
                own[s * (pz // pf) + h, j] = rows.astype(jnp.bfloat16)

        @pl.when(j + SLOTS < bins)
        def _():
            fetch(kern, kbuf, ksem, j + SLOTS).start()

    def iteration(i, carry):
        @pl.when(i < count)
        def _():
            settle(gat.at[z, pl.ds(0, nf - 1), part(i)], a_recv.at[i])
            pass_on(z, i, True)
            pass_on(z, i, False)

        for d in range(1, nz):
            c = i - LAG * d

            @pl.when((c >= 0) & (c < count) & (z - d >= 0))
            def _():
                settle(gat.at[z - d, :, part(c)], z_recv.at[z - d, c])
                pass_on(z - d, c, True)

            @pl.when((c >= 0) & (c < count) & (z + d < nz))
            def _():
                settle(gat.at[z + d, :, part(c)], z_recv.at[z + d, c])
                pass_on(z + d, c, False)

        c = i - LAG * (nz - 1)

        @pl.when((c >= 0) & (c < count))
        def _():
            for k in range(chunk):
                multiply(c * chunk + k)
            pltpu.make_async_copy(own.at[f, part(c)], out.at[f, part(c)], osem).start()
            for step in range(1, nf):
                t = lax.rem(f + step, nf)
                remote(
                    own.at[t, part(c)], out.at[f, part(c)], w_send.at[step], w_recv.at[step], "freq", t
                ).start()

        return carry

    lax.fori_loop(0, count + LAG * (nz - 1), iteration, 0)
    settle(out.at[f], osem)
    for step in range(1, nf):
        settle(out.at[lax.rem(f + nf - step, nf)], w_recv.at[step])
        settle(own.at[lax.rem(f + step, nf)], w_send.at[step])
        settle(spec.at[lax.rem(f + step, nf)], a_send.at[step])
    for s in range(nz):

        @pl.when((s <= z) & (z < nz - 1))
        def _():
            settle(gat.at[s], z_send.at[0, s])

        @pl.when((s >= z) & (z > 0))
        def _():
            settle(gat.at[s], z_send.at[1, s])


def terms_kernel(
    nf, nz, pz, pf, back, kern, out, held, term, left, right, total, kbuf, ksem, lsem, osem,
    h_send, h_recv, z_send, z_recv, w_send, w_recv
):
    f, z = lax.axis_index("freq"), lax.axis_index("src")
    bins = back.shape[1]
    rl = out.shape[3]
    chunk = chunk_bins(bins)
    count = bins // chunk
    half = nf * pf

    def part(c):
        return pl.ds(c * chunk, chunk)

    for j in range(SLOTS):
        fetch(kern, kbuf, ksem, j).start()
    mine = pltpu.make_async_copy(back.at[f], held.at[f], lsem)
    mine.start()

    @pl.when(z == 0)
    def _():
        left[0] = jnp.zeros(left.shape[1:], left.dtype)

    @pl.when(z == nz - 1)
    def _():
        right[nz - 1] = jnp.zeros(right.shape[1:], right.dtype)

    enter(f, z, nf, nz)

    def scatter(c, carry):
        for step in range(1, nf):
            t = lax.rem(f + step, nf)
            remote(
                back.at[t, part(c)], held.at[f, part(c)], h_send.at[step], h_recv.at[c], "freq", t
            ).start()
        return carry

    lax.fori_loop(0, count, scatter, 0)
    mine.wait()

    def multiply(j):
        fetch(kern, kbuf, ksem, j).wait()
        slot = lax.rem(j, SLOTS)
        each = [held[r, j].astype(jnp.float32) for r in range(nf)]
        x = jnp.concatenate([e[:pf] for e in each] + [e[pf:] for e in each], axis=0).astype(jnp.bfloat16)
        a = lax.dot_general(x, kbuf[slot, 0], NN, preferred_element_type=jnp.float32)
        b = lax.dot_general(x, kbuf[slot, 1], NN, preferred_element_type=jnp.float32)
        real = a[:half] + b[half:]
        imag = a[half:] - b[:half]
        for s in range(nz):
            rows = jnp.concatenate([real[s * pz : (s + 1) * pz], imag[s * pz : (s + 1) * pz]], axis=0)
            rows = rows.astype(jnp.bfloat16)
            for r in range(nf):
                term[s, j, r] = rows[:, r * rl : (r + 1) * rl]

        @pl.when(j + SLOTS < bins)
        def _():
            fetch(kern, kbuf, ksem, j + SLOTS).start()

    def add(d, c, held_sum):
        summed = term[d, part(c)].astype(jnp.float32) + held_sum[d, part(c)].astype(jnp.float32)
        term[d, part(c)] = summed.astype(jnp.bfloat16)

    def iteration(i, carry):
        @pl.when(i < count)
        def _():
            settle(held.at[pl.ds(0, nf - 1), part(i)], h_recv.at[i])
            for k in range(chunk):
                multiply(i * chunk + k)

        c0 = i - LAG * z
        c1 = i - LAG * (nz - 1 - z)
        for d in range(nz - 1, 0, -1):

            @pl.when((c0 >= 0) & (c0 < count) & (z < d))
            def _():
                @pl.when(z > 0)
                def _():
                    settle(left.at[d, part(c0)], z_recv.at[0, d, c0])
                    add(d, c0, left)

                remote(
                    term.at[d, part(c0)], left.at[d, part(c0)], z_send.at[d], z_recv.at[0, d, c0], "src", z + 1
                ).start()

        for d in range(nz - 1):

            @pl.when((c1 >= 0) & (c1 < count) & (z > d))
            def _():
                @pl.when(z < nz - 1)
                def _():
                    settle(right.at[d, part(c1)], z_recv.at[1, d, c1])
                    add(d, c1, right)

                remote(
                    term.at[d, part(c1)], right.at[d, part(c1)], z_send.at[d], z_recv.at[1, d, c1], "src", z - 1
                ).start()

        c = i - LAG * jnp.maximum(z, nz - 1 - z)

        @pl.when((c >= 0) & (c < count))
        def _():
            @pl.when(z > 0)
            def _():
                settle(left.at[z, part(c)], z_recv.at[0, z, c])

            @pl.when(z < nz - 1)
            def _():
                settle(right.at[z, part(c)], z_recv.at[1, z, c])

            summed = (
                term[z, part(c)].astype(jnp.float32)
                + left[z, part(c)].astype(jnp.float32)
                + right[z, part(c)].astype(jnp.float32)
            ).astype(jnp.bfloat16)
            for r in range(nf):
                total[r, part(c)] = summed[:, r]
            pltpu.make_async_copy(total.at[f, part(c)], out.at[f, part(c)], osem).start()
            for step in range(1, nf):
                t = lax.rem(f + step, nf)
                remote(
                    total.at[t, part(c)], out.at[f, part(c)], w_send.at[step], w_recv.at[step], "freq", t
                ).start()

        return carry

    lax.fori_loop(0, count + LAG * (nz - 1), iteration, 0)
    settle(out.at[f], osem)
    for step in range(1, nf):
        settle(out.at[lax.rem(f + nf - step, nf)], w_recv.at[step])
        settle(total.at[lax.rem(f + step, nf)], w_send.at[step])
        settle(back.at[lax.rem(f + step, nf)], h_send.at[step])
    for d in range(nz):

        @pl.when(d != z)
        def _():
            settle(term.at[d], z_send.at[d])


def local(nf, nz, focusing, direct, kernel, onset_up, onset_back):
    pz, rl, nt = focusing.shape
    _, bins, sl, receivers = kernel.shape
    pf = onset_up.shape[0]
    forward, inverse = band_tables(nt, nf * bins)
    forward, inverse = jnp.asarray(forward), jnp.asarray(inverse)
    sample_index = jnp.arange(nt, dtype=jnp.int32)
    count = bins // chunk_bins(bins)
    anywhere = pl.BlockSpec(memory_space=pl.ANY)
    dma = pltpu.SemaphoreType.DMA
    vmem = lambda *shape: pltpu.VMEM(shape, jnp.bfloat16)
    params = lambda n: pltpu.CompilerParams(vmem_limit_bytes=40 << 20, collective_id=n, has_side_effects=True)
    common = [vmem(SLOTS, 2, sl, receivers), dma((SLOTS,)), dma, dma, dma((nf,)), dma((count,))]
    cost = pl.CostEstimate(
        flops=8 * bins * sl * receivers * nf * pf,
        bytes_accessed=4 * bins * sl * receivers,
        transcendentals=0,
    )

    spectrum = jnp.einsum("kt,prt->kpr", forward, focusing, preferred_element_type=jnp.float32)
    spectrum = spectrum.astype(jnp.bfloat16).reshape(nf, bins, 2 * pz, rl)
    timed = pl.pallas_call(
        lambda *refs: waves_kernel(nf, nz, pz, pf, *refs),
        out_shape=jax.ShapeDtypeStruct((nf, bins, 2 * pf, sl), jnp.bfloat16),
        in_specs=[anywhere, anywhere],
        out_specs=anywhere,
        scratch_shapes=[vmem(nz, nf, bins, 2 * pz, rl), vmem(nf, bins, 2 * pf, sl)]
        + common
        + [dma((2, nz)), dma((nz, count)), dma((nf,)), dma((nf,))],
        compiler_params=params(0),
        cost_estimate=cost,
        name="waves",
    )(spectrum, kernel)
    signal = jnp.einsum(
        "kps,kt->pst",
        timed.reshape(2 * nf * bins, pf, sl),
        inverse,
        preferred_element_type=jnp.float32,
    )
    upgoing = jnp.where(sample_index[None, None, :] < onset_up[:, :, None], signal, 0.0).astype(
        jnp.bfloat16
    )
    back = jnp.einsum("kt,pst->kps", forward, upgoing, preferred_element_type=jnp.float32)
    back = back.astype(jnp.bfloat16).reshape(nf, bins, 2 * pf, sl)
    spread = pl.pallas_call(
        lambda *refs: terms_kernel(nf, nz, pz, pf, *refs),
        out_shape=jax.ShapeDtypeStruct((nf, bins, 2 * pz, rl), jnp.bfloat16),
        in_specs=[anywhere, anywhere],
        out_specs=anywhere,
        scratch_shapes=[vmem(nf, bins, 2 * pf, sl)]
        + [vmem(nz, bins, nf, 2 * pz, rl)] * 3
        + [vmem(nf, bins, 2 * pz, rl)]
        + common
        + [dma((nz,)), dma((2, nz, count)), dma((nf,)), dma((nf,))],
        compiler_params=params(1),
        cost_estimate=cost,
        name="terms",
    )(back, kernel)
    trace = jnp.einsum(
        "kpr,kt->prt",
        spread.reshape(2 * nf * bins, pz, rl),
        inverse,
        preferred_element_type=jnp.float32,
    )
    cut = jnp.where(sample_index[None, None, :] < onset_back[:, :, None], trace, 0.0)
    updated = (direct.astype(jnp.float32) - cut).astype(jnp.bfloat16)
    return (upgoing, updated)


def solution(mesh):
    placed = (
        P("src", "freq", None),
        P("src", "freq", None),
        P(None, "freq", "src", None),
        P("freq", "src"),
        P("src", "freq"),
    )
    nf, nz = mesh.shape["freq"], mesh.shape["src"]
    return jax.shard_map(
        lambda *args: local(nf, nz, *args),
        mesh=mesh,
        in_specs=placed,
        out_specs=(P("freq", "src", None), P("src", "freq", None)),
        check_vma=False,
    )
```

time: 302 us -> 159 us (0.53)
  waiting for transfers between devices: 120 us -> 0 us
  blocking collectives: 81.7 us -> 0 us
  Pallas kernels: 59.4 us -> 137 us
  between operations: 14.1 us -> 0.79 us
    all_to_all x4 -> x0, blocking collectives: 81.7 us -> none  [the longest x1 24.4 us: local(): lax.all_to_all(waves, 'freq', split_axis=0, concat_axis=0, tiled=True)]
    pallas_call x2, Pallas kernels: 59.4 us -> 137 us  [the longest x1 69 us: local(): pl.pallas_call(lambda *refs: terms_kernel(nf, nz, pz, pf, *refs), out_sha...]
    all_gather x1 -> x0, waiting for transfers between devices: 63 us -> none  [local(): gathered = lax.all_gather(grouped, 'src', axis=0, tiled=False)]
    reduce_scatter x1 -> x0, waiting for transfers between devices: 57.2 us -> none  [local(): summed = lax.psum_scatter(terms, 'src', scatter_dimension=0, tiled=False)]
  transfers between devices with their start and end apart: 2 -> 0, of which waited for: 2 -> 0; matrix products, arithmetic and copies ran while one was open for 0% -> 0% of each run, Pallas kernels for 0% -> 0%
where the time goes in v2:
time: 159 us
  Pallas kernels  137 us (86%)
  matrix products  19.2 us (12%)
  local copies, waits for them, and re-layouts  2.61 us (2%)
    pallas_call x1, Pallas kernels, local(): pl.pallas_call(lambda *refs: terms_kernel(nf, nz, pz, pf, *refs), out_sha...  69 us
    pallas_call x1, Pallas kernels, local(): pl.pallas_call(lambda *refs: waves_kernel(nf, nz, pz, pf, *refs), out_sha...  67.7 us
    dot_general x1, matrix products, local(): jnp.einsum('kps,kt->pst', timed.reshape(2 * nf * bins, pf, sl), inverse,...  6.56 us
    dot_general x1, matrix products, local(): jnp.einsum('kpr,kt->prt', spread.reshape(2 * nf * bins, pz, rl), inverse,...  4.67 us
    dot_general x1, matrix products, local(): jnp.einsum('kt,prt->kpr', forward, focusing, preferred_element_type=jnp.f...  4.49 us
    dot_general x1, matrix products, local(): jnp.einsum('kt,pst->kps', forward, upgoing, preferred_element_type=jnp.fl...  3.44 us

profile of v2, /device:TPU:0, one launch (start us, length us, event | category | flops | bytes accessed | tf_op | source)
XLA Modules:
  0.0 159.3 jit_solution(6793544749843964832)
XLA Ops:
  0.6 4.5 %convolution_convert_fusion.1 = bf16[384,8,128]{2,0,1:T(8,128)(2,1)S(1)} fusion(bf16[384,2048,1]{1,0,2:T(8,128)(2,1)} %constant.9, bf16[8,128,2048]{2,1,0:T(8,128)(2,1)} %param.7), kind=kOutput, calls=%fused_computation.7 | convolution fusion | flops 1611005952 | bytes 6553600 | tf_op jit(solution)/shard_map/kt,prt->kpr/dot_general | solution.py:337
  5.1 0.5 copy.9
  5.6 0.0 copy-start.1
  5.7 67.7 %waves.1 = bf16[8,24,8,512]{3,2,1,0:T(8,128)(2,1)S(1)} custom-call(bf16[8,24,16,128]{3,2,1,0:T(8,128)(2,1)S(1)} %bitcast.14, bf16[2,24,512,1024]{3,2,1,0:T(8,128)(2,1)} %refs_1_.3), custom_call_target="tpu_custom_call" | custom-call | flops 3221225472 | bytes 50331648 | tf_op jit(solution)/shard_map/waves/pallas_call | solution.py:339
  73.4 0.4 reshape.19
  73.8 0.0 copy-done.1
  73.8 0.0 copy-start.5
  73.8 6.6 %select_convert_fusion = bf16[4,512,2048]{2,1,0:T(8,128)(2,1)S(1)} fusion(s32[4,512]{1,0:T(4,128)S(1)} %copy-done.1, bf16[384,2048,1]{1,0,2:T(8,128)(2,1)} %constant.10, bf16[384,4,512]{2,1,0:T(4,128)(2,1)S(1)} %reshape.19), kind=kOutput, calls=%fused_computation | convolution fusion | flops 3233808384 | bytes 11542528 | tf_op jit(solution)/shard_map/kps,kt->pst/dot_general | solution.py:351
  80.4 0.0 copy-done.5
  80.4 0.0 copy-start.3
  80.4 3.4 %fusion.1 = bf16[384,4,512]{2,0,1:T(8,128)(2,1)S(1)} fusion(bf16[4,512,2048]{2,1,0:T(8,128)(2,1)S(1)} %select_convert_fusion, bf16[384,2048,1]{1,0,2:T(8,128)(2,1)S(1)} %copy-done.5), kind=kOutput, calls=%fused_computation.6 | convolution fusion | flops 3222011904 | bytes 11534336 | tf_op jit(solution)/shard_map/kt,pst->kps/dot_general | solution.py:360
  83.8 0.0 copy-done.3
  83.9 1.2 copy.11
  85.1 0.4 reshape.20.refs_0_
  85.5 0.0 copy-start
  85.5 0.0 copy-start.2
  85.5 0.0 copy-start.4
  85.5 69.0 %terms.1 = bf16[8,24,16,128]{3,2,1,0:T(8,128)(2,1)S(1)} custom-call(bf16[8,24,8,512]{3,2,1,0:T(8,128)(2,1)S(1)} %reshape.20.refs_0_, bf16[2,24,512,1024]{3,2,1,0:T(8,128)(2,1)} %refs_1_.3), custom_call_target="tpu_custom_call" | custom-call | flops 3221225472 | bytes 50331648 | tf_op jit(solution)/shard_map/terms/pallas_call | solution.py:362
  154.6 0.0 copy-done
  154.6 0.0 copy-done.2
  154.6 0.0 copy-done.4
  154.6 4.7 %subtract_convert_fusion = bf16[8,128,2048]{2,1,0:T(8,128)(2,1)} fusion(bf16[8,128,2048]{2,1,0:T(8,128)(2,1)S(1)} %copy-done, bf16[384,2048,1]{1,0,2:T(8,128)(2,1)S(1)} %copy-done.4, s32[8,128]{1,0:T(8,128)S(1)} %copy-done.2, bf16[384,8,128]{2,1,0:T(8,128)(2,1)S(1)} %bitcast.15), kind=kOutput, calls=%fused_computation.2 | convolution fusion | flops 1621098496 | bytes 10752000 | tf_op jit(solution)/shard_map/kpr,kt->prt/dot_general | solution.py:376
Async XLA Ops:
  5.6 68.1 %copy-start.1 = (s32[4,512]{1,0:T(4,128)S(1)}, s32[4,512]{1,0:T(4,128)}, u32[]{:S(2)}) copy-start(s32[4,512]{1,0:T(4,128)} %param.10) | copy-start | bytes 24580
  73.8 6.6 %copy-start.5 = (bf16[384,2048,1]{1,0,2:T(8,128)(2,1)S(1)}, bf16[384,2048,1]{1,0,2:T(8,128)(2,1)}, u32[]{:S(2)}) copy-start(bf16[384,2048,1]{1,0,2:T(8,128)(2,1)} %constant.9) | copy-start | bytes 4718596
  80.4 3.5 %copy-start.3 = (bf16[4,512,2048]{2,1,0:T(8,128)(2,1)}, bf16[4,512,2048]{2,1,0:T(8,128)(2,1)S(1)}, u32[]{:S(2)}) copy-start(bf16[4,512,2048]{2,1,0:T(8,128)(2,1)S(1)} %select_convert_fusion) | copy-start | bytes 25165828
  85.5 69.1 %copy-start = (bf16[8,128,2048]{2,1,0:T(8,128)(2,1)S(1)}, bf16[8,128,2048]{2,1,0:T(8,128)(2,1)}, u32[]{:S(2)}) copy-start(bf16[8,128,2048]{2,1,0:T(8,128)(2,1)} %param.8) | copy-start | bytes 12582916
  85.5 69.1 %copy-start.2 = (s32[8,128]{1,0:T(8,128)S(1)}, s32[8,128]{1,0:T(8,128)}, u32[]{:S(2)}) copy-start(s32[8,128]{1,0:T(8,128)} %param.11) | copy-start | bytes 12292
  85.5 69.1 %copy-start.4 = (bf16[384,2048,1]{1,0,2:T(8,128)(2,1)S(1)}, bf16[384,2048,1]{1,0,2:T(8,128)(2,1)}, u32[]{:S(2)}) copy-start(bf16[384,2048,1]{1,0,2:T(8,128)(2,1)} %constant.10) | copy-start | bytes 4718596
